TPU v7x, 512 devices: a whole 4x4x16 slice. The times are simulated.
512 devices in a mesh: energy: 64 (over x, z), slab: 8 (over y, core).
Axes of the slice: x: 4, y: 4, z: 16, core: 2. Of those that a mesh axis runs over, the one named last changes fastest.
Arguments:
- green_block: bfloat16 [64, 8, 2, 192, 192], P('energy', 'slab'), may hold values from -0.4375 to 0.4375
- coupling: bfloat16 [64, 8, 2, 192, 192], P('energy', 'slab'), may hold values from -0.4375 to 0.4375
- sigma_lesser: bfloat16 [64, 8, 2, 192, 192], P('energy', 'slab'), may hold values from -6 to 6
- screened: bfloat16 [8, 2, 128, 36864], P('slab', None, None, 'energy'), may hold values from -9 to 9
Outputs:
- sigma_next: bfloat16 [64, 8, 2, 192, 192], P('energy', 'slab')
All inputs are finite; a program needn't handle non-finite values.
Results may differ from a plain program's by a relative error of at most 0.0049.
Values may be sent and summed in bfloat16 or wider, within the bound.
No kernel may reach another device: no remote copies, remote signals or barrier semaphores. Data moves between devices by JAX's collectives and lax.ppermute only.
A program may use at most 128 MiB of HBM per device.

v0:
```python
import math
import jax
import jax.numpy as jnp
from jax import lax
from jax.sharding import PartitionSpec as P


def from_behind(value, axis, steps):
    count = lax.axis_size(axis)
    first, last = (max(0, -steps), min(count, count - steps))
    return lax.ppermute(value, axis, [(source, source + steps) for source in range(first, last)])


def product(form, first, second):
    return jnp.einsum(form, first, second, preferred_element_type=jnp.float32)


def sandwich(outer, inner):
    outer_real = outer[:, 0]
    outer_imag = outer[:, 1]
    inner_real = inner[:, 0]
    inner_imag = inner[:, 1]
    forward = "eij,ejk->eik"
    adjoint = "eik,ejk->eij"
    half_real = (
        product(forward, outer_real, inner_real) - product(forward, outer_imag, inner_imag)
    ).astype(jnp.bfloat16)
    half_imag = (
        product(forward, outer_real, inner_imag) + product(forward, outer_imag, inner_real)
    ).astype(jnp.bfloat16)
    full_real = product(adjoint, half_real, outer_real) + product(adjoint, half_imag, outer_imag)
    full_imag = product(adjoint, half_imag, outer_real) - product(adjoint, half_real, outer_imag)
    return jnp.stack([full_real, full_imag], axis=1)


def stacked_tables(count):
    length = 2 * count
    rows = jnp.arange(length, dtype=jnp.int32)
    cols = jnp.arange(count, dtype=jnp.int32)
    phases = rows[:, None] * cols[None, :] % length
    angles = phases.astype(jnp.float32) * (2.0 * math.pi / length)
    cosine = jnp.cos(angles)
    sine = jnp.sin(angles)
    from_real = jnp.concatenate([cosine, -sine], axis=0)
    from_imag = jnp.concatenate([sine, cosine], axis=0)
    forward = jnp.stack([from_real, from_imag], axis=-1).reshape(2 * length, 2 * count)
    to_real = jnp.concatenate([cosine.T, -sine.T], axis=1)
    to_imag = jnp.concatenate([sine.T, cosine.T], axis=1)
    backward = jnp.stack([to_real, to_imag], axis=1).reshape(2 * count, 2 * length)
    return (forward, backward)


def shards(green_block, coupling, sigma_lesser, screened):
    high = lax.Precision.HIGHEST
    green_here = green_block[:, 0]
    couple_here = coupling[:, 0]
    sigma_here = sigma_lesser[:, 0]
    energies_here = green_here.shape[0]
    orbitals = green_here.shape[2]
    own_term = sandwich(green_here, sigma_here)
    couple_before = from_behind(couple_here, "slab", 1)
    made_term = sandwich(couple_before, sigma_here)
    far_term = from_behind(made_term, "slab", -1)
    lesser = (own_term + far_term).reshape(energies_here, 2, orbitals * orbitals)
    columns = lax.all_to_all(lesser, "energy", split_axis=2, concat_axis=0, tiled=True)
    total_energies = columns.shape[0]
    width = columns.shape[2]
    length = 2 * total_energies
    forward, backward = stacked_tables(total_energies)
    stacked = columns.reshape(2 * total_energies, width)
    spectrum = jnp.dot(forward, stacked, precision=high)
    spec_real = spectrum[:length]
    spec_imag = spectrum[length:]
    screen_real = screened[0, 0].astype(jnp.float32)
    screen_imag = screened[0, 1].astype(jnp.float32)
    conv_real = spec_real * screen_real - spec_imag * screen_imag
    conv_imag = spec_real * screen_imag + spec_imag * screen_real
    convolved = jnp.concatenate([conv_real, conv_imag], axis=0)
    back = jnp.dot(backward, convolved, precision=high)
    joined = (back.reshape(total_energies, 2, width) / length).astype(jnp.bfloat16)
    returned = lax.all_to_all(joined, "energy", split_axis=0, concat_axis=2, tiled=True)
    return returned.reshape(energies_here, 1, 2, orbitals, orbitals)


def solution(mesh):
    placed = (
        P("energy", "slab", None, None, None),
        P("energy", "slab", None, None, None),
        P("energy", "slab", None, None, None),
        P("slab", None, None, "energy"),
    )
    return jax.shard_map(
        shards,
        mesh=mesh,
        in_specs=placed,
        out_specs=P("energy", "slab", None, None, None),
        check_vma=False,
    )
```

profile of v0, /device:TPU:22, one launch (start us, length us, event | category | flops | bytes accessed | tf_op | source)
XLA Modules:
  0.0 324.2 jit_solution(17223660874348334574)
XLA Ops:
  0.0 1.9 collective-permute-start
  1.9 1.1 fusion.17
  3.0 1.1 fusion.19
  4.1 1.1 fusion.6
  5.3 1.1 fusion.5
  6.4 1.1 fusion.16
  7.5 1.1 fusion.20
  8.5 1.1 fusion.21
  9.6 1.1 fusion.8
  10.9 1.1 fusion.7
  12.1 0.2 fusion.2
  12.4 0.2 fusion.1
  12.6 3.6 %collective-permute-start.1 = (f32[1,2,192,192]{3,2,1,0:T(8,128)S(1)}, f32[1,2,192,192]{3,2,1,0:T(8,128)S(1)}, u32[]{:S(2)}, u32[]{:S(2)}) collective-permute-start(f32[1,2,192,192]{3,2,1,0:T(8,128)S(1)} %pad_maximum_fusion), channel_id=1, source_target_pairs={{1,0},{2,1},{3,2},{4,3},{5,4},{6,5},{7,6},{9,8},{10,9},{11,10},{12... | collective-permute-start | bytes 884744 | tf_op jit(solution)/shard_map/ppermute | solution.py:11
  16.2 1.1 fusion.18
  17.3 1.1 fusion.3
  18.4 1.1 fusion.4
  19.6 2.0 collective-permute-done.1
  21.6 9.7 %copy.19 = f32[1,2,192,192]{1,3,2,0:T(8,128)} copy(f32[1,2,192,192]{3,2,1,0:T(8,128)S(1)} %maximum_add_fusion) | data formatting | bytes 589824 | tf_op jit(solution)/shard_map/reshape | solution.py:64
  31.3 0.5 broadcast.37
  31.8 164.6 %reduce = f32[36864,2]{1,0:T(8,128)} reduce(f32[36864,1,2]{2,1,0:T(1,128)} %bitcast.90, f32[]{:T(128)} %broadcast.37), dimensions={1}, to_apply=%bitcast.78.reduce_sub_computation | reduce | bytes 589828
  196.4 16.0 %reshape.143 = f32[64,1,1152]{2,1,0:T(1,128)} reshape(f32[36864,2]{1,0:T(8,128)} %reduce) | data formatting | bytes 589824
  212.4 18.8 %all-to-all-start = ((f32[64,1,1152]{2,1,0:T(1,128)}), f32[64,1,1152]{2,1,0:T(1,128)S(1)}, u32[]{:S(2)}, u32[]{:S(2)}) async-start(f32[64,1,1152]{2,1,0:T(1,128)} %reshape.143), calls=%async_computation | async-start | bytes 589824 | tf_op jit(solution)/shard_map/all_to_all | solution.py:65
  232.2 21.7 %all-to-all-done = f32[64,1,1152]{2,1,0:T(1,128)S(1)} async-done(((f32[64,1,1152]{2,1,0:T(1,128)}), f32[64,1,1152]{2,1,0:T(1,128)S(1)}, u32[]{:S(2)}, u32[]{:S(2)}) %all-to-all-start) | async-done | bytes 294944 | tf_op jit(solution)/shard_map/all_to_all | solution.py:65
  254.0 1.3 reduce.1
  255.3 30.6 %reshape.144 = f32[36864,1,2]{2,1,0:T(1,128)} reshape(f32[64,1152]{1,0:T(8,128)S(1)} %reduce.1) | data formatting | bytes 589824
  285.9 11.1 %copy.20 = f32[1,2,64,576]{3,2,1,0:T(8,128)S(1)} copy(f32[1,2,64,576]{1,3,2,0:T(8,128)} %bitcast.91) | data formatting | bytes 589824 | tf_op jit(solution)/shard_map/all_to_all | solution.py:65
  297.0 0.3 copy.16
  297.2 0.2 reshape.138
  297.5 0.7 fusion.43
  298.3 0.7 fusion
  299.2 24.1 %all_to_all.30 = bf16[64,2,576]{2,1,0:T(2,128)(2,1)S(1)} all-to-all(bf16[64,2,576]{2,1,0:T(2,128)(2,1)S(1)} %copy.17), channel_id=1, replica_groups=mesh['energy'=64,'slab'=8] {'energy'}, dimensions={0} | all-to-all | bytes 294912 | tf_op jit(solution)/shard_map/all_to_all | solution.py:81
  323.4 0.9 reshape.139
  (20 shorter events, 1.7 us)
Async XLA Ops:
  0.0 7.5 %collective-permute-start = (bf16[1,2,192,192]{3,2,1,0:T(8,128)(2,1)}, bf16[1,2,192,192]{3,2,1,0:T(8,128)(2,1)S(1)}, u32[]{:S(2)}, u32[]{:S(2)}) collective-permute-start(bf16[1,2,192,192]{3,2,1,0:T(8,128)(2,1)} %bitcast.110), channel_id=1, source_target_pairs={{0,1},{1,2},{2,3},{3,4},{4,5},{5,6},{6,7},{8,9},{9,10},{10,11},{11... | collective-permute-start | bytes 442376 | tf_op jit(solution)/shard_map/ppermute | solution.py:11
  12.6 8.9 %collective-permute-start.1 = (f32[1,2,192,192]{3,2,1,0:T(8,128)S(1)}, f32[1,2,192,192]{3,2,1,0:T(8,128)S(1)}, u32[]{:S(2)}, u32[]{:S(2)}) collective-permute-start(f32[1,2,192,192]{3,2,1,0:T(8,128)S(1)} %pad_maximum_fusion), channel_id=1, source_target_pairs={{1,0},{2,1},{3,2},{4,3},{5,4},{6,5},{7,6},{9,8},{10,9},{11,10},{12... | collective-permute-start | bytes 884744 | tf_op jit(solution)/shard_map/ppermute | solution.py:11
  212.4 41.5 %all-to-all-start = ((f32[64,1,1152]{2,1,0:T(1,128)}), f32[64,1,1152]{2,1,0:T(1,128)S(1)}, u32[]{:S(2)}, u32[]{:S(2)}) async-start(f32[64,1,1152]{2,1,0:T(1,128)} %reshape.143), calls=%async_computation | async-start | bytes 589824 | tf_op jit(solution)/shard_map/all_to_all | solution.py:65
  255.3 42.9 %copy-start = (bf16[1,2,128,576]{2,3,1,0:T(8,128)(2,1)S(1)}, bf16[1,2,128,576]{2,3,1,0:T(8,128)(2,1)}, u32[]{:S(2)}) copy-start(bf16[1,2,128,576]{2,3,1,0:T(8,128)(2,1)} %param.7) | copy-start | bytes 884740
where the time goes:
time: 325 us; the launch traced here: 324 us
  other arithmetic  167 us (51%)
  local copies, waits for them, and re-layouts  69.6 us (21%)
  starting transfers between devices  24.3 us (7%)
  blocking collectives  24.1 us (7%)
  waiting for transfers between devices  23.7 us (7%)
  matrix products  15.4 us (5%)
    unnamed x1, other arithmetic  165 us
    unnamed x5, local copies, waits for them, and re-layouts  47.1 us
    all_to_all x1, blocking collectives, shards(): lax.all_to_all(joined, 'energy', split_axis=0, concat_axis=2, tiled=True)  24.1 us
    all_to_all x1, waiting for transfers between devices, shards(): lax.all_to_all(lesser, 'energy', split_axis=2, concat_axis=0, tiled=True)  21.7 us
    all_to_all x1, starting transfers between devices, shards(): lax.all_to_all(lesser, 'energy', split_axis=2, concat_axis=0, tiled=True)  18.8 us
    dot_general x16, matrix products, product(): return jnp.einsum(form, first, second, preferred_element_type=jnp.float32)  13.9 us
    all_to_all x2, local copies, waits for them, and re-layouts, shards(): lax.all_to_all(lesser, 'energy', split_axis=2, concat_axis=0, tiled=True)  11.3 us
    reshape x1, local copies, waits for them, and re-layouts, shards(): (own_term + far_term).reshape(energies_here, 2, orbitals * orbitals)  9.69 us
  transfers between devices with their start and end apart: 3, of which 2 were waited for; matrix products, arithmetic and copies ran while one was open for 3% of the time, Pallas kernels for 0%

commit v1 on v0

--- a/solution.py
+++ b/solution.py
@@ -62,7 +62,12 @@
     made_term = sandwich(couple_before, sigma_here)
     far_term = from_behind(made_term, "slab", -1)
     lesser = (own_term + far_term).reshape(energies_here, 2, orbitals * orbitals)
-    columns = lax.all_to_all(lesser, "energy", split_axis=2, concat_axis=0, tiled=True)
+    columns = jnp.concatenate(
+        lax.all_to_all(
+            jnp.stack(jnp.split(lesser, lax.axis_size("energy"), axis=2)), "energy", 0, 0
+        ),
+        axis=0,
+    )
     total_energies = columns.shape[0]
     width = columns.shape[2]
     length = 2 * total_energies

time: 325 us -> 127 us (0.39)
  other arithmetic: 167 us -> 0.88 us
  local copies, waits for them, and re-layouts: 69.6 us -> 42.2 us
  matrix products: 15.4 us -> 5.42 us
  waiting for transfers between devices: 23.7 us -> 31.1 us
    unnamed x1 -> x0, other arithmetic: 165 us -> none
    all_to_all x2 -> x0, local copies, waits for them, and re-layouts: 11.3 us -> none  [shards(): lax.all_to_all(lesser, 'energy', split_axis=2, concat_axis=0, tiled=True)]
    dot_general x16, matrix products: 13.9 us -> 3.94 us  [product(): return jnp.einsum(form, first, second, preferred_element_type=jnp.float32)]
    reshape x1, local copies, waits for them, and re-layouts: 9.69 us -> 0.3 us  [shards(): (own_term + far_term).reshape(energies_here, 2, orbitals * orbitals)]
    unnamed x5 -> x69, local copies, waits for them, and re-layouts: 47.1 us -> 39.8 us
    ppermute x2, waiting for transfers between devices: 1.98 us -> 8.01 us  [from_behind(): lax.ppermute(value, axis, [(source, source + steps) for source in range(f...]
  transfers between devices with their start and end apart: 3 -> 3, of which waited for: 2 -> 3; matrix products, arithmetic and copies ran while one was open for 3% -> 3% of each run, Pallas kernels for 0% -> 0%
where the time goes in v1:
time: 127 us
  local copies, waits for them, and re-layouts  42.2 us (33%)
  waiting for transfers between devices  31.1 us (24%)
  blocking collectives  24.2 us (19%)
  starting transfers between devices  22.6 us (18%)
  matrix products  5.42 us (4%)
    unnamed x69, local copies, waits for them, and re-layouts  39.8 us
    all_to_all x1, blocking collectives, shards(): lax.all_to_all(joined, 'energy', split_axis=0, concat_axis=2, tiled=True)  24.2 us
    all_to_all x1, waiting for transfers between devices, shards(): lax.all_to_all(jnp.stack(jnp.split(lesser, lax.axis_size('energy'), axis=...  23.1 us
    all_to_all x1, starting transfers between devices, shards(): lax.all_to_all(jnp.stack(jnp.split(lesser, lax.axis_size('energy'), axis=...  18.8 us
    ppermute x2, waiting for transfers between devices, from_behind(): lax.ppermute(value, axis, [(source, source + steps) for source in range(f...  8.01 us
    dot_general x16, matrix products, product(): return jnp.einsum(form, first, second, preferred_element_type=jnp.float32)  3.94 us
    ppermute x2, starting transfers between devices, from_behind(): lax.ppermute(value, axis, [(source, source + steps) for source in range(f...  3.83 us
  transfers between devices with their start and end apart: 3, of which 3 were waited for; matrix products, arithmetic and copies ran while one was open for 3% of the time, Pallas kernels for 0%

profile of v1, /device:TPU:22, one launch (start us, length us, event | category | flops | bytes accessed | tf_op | source)
XLA Modules:
  0.0 126.7 jit_solution(16834738504822294628)
XLA Ops:
  0.0 1.9 %collective-permute-start = (bf16[1,2,192,192]{3,2,1,0:T(8,128)(2,1)}, bf16[1,2,192,192]{3,2,1,0:T(8,128)(2,1)S(1)}, u32[]{:S(2)}, u32[]{:S(2)}) collective-permute-start(bf16[1,2,192,192]{3,2,1,0:T(8,128)(2,1)} %bitcast.358), channel_id=1, source_target_pairs={{0,1},{1,2},{2,3},{3,4},{4,5},{5,6},{6,7},{8,9},{9,10},{10,11},{11... | collective-permute-start | bytes 442376 | tf_op jit(solution)/shard_map/ppermute | solution.py:11
  1.9 1.1 fusion.17
  3.8 3.4 %collective-permute-done = bf16[1,2,192,192]{3,2,1,0:T(8,128)(2,1)S(1)} collective-permute-done((bf16[1,2,192,192]{3,2,1,0:T(8,128)(2,1)}, bf16[1,2,192,192]{3,2,1,0:T(8,128)(2,1)S(1)}, u32[]{:S(2)}, u32[]{:S(2)}) %collective-permute-start) | collective-permute-done | bytes 147488 | tf_op jit(solution)/shard_map/ppermute | solution.py:11
  8.7 1.9 %collective-permute-start.1 = (f32[1,2,192,192]{3,2,1,0:T(8,128)S(1)}, f32[1,2,192,192]{3,2,1,0:T(8,128)S(1)}, u32[]{:S(2)}, u32[]{:S(2)}) collective-permute-start(f32[1,2,192,192]{3,2,1,0:T(8,128)S(1)} %pad_maximum_fusion), channel_id=1, source_target_pairs={{1,0},{2,1},{3,2},{4,3},{5,4},{6,5},{7,6},{9,8},{10,9},{11,10},{12... | collective-permute-start | bytes 884744 | tf_op jit(solution)/shard_map/ppermute | solution.py:11
  11.3 4.7 %collective-permute-done.1 = f32[1,2,192,192]{3,2,1,0:T(8,128)S(1)} collective-permute-done((f32[1,2,192,192]{3,2,1,0:T(8,128)S(1)}, f32[1,2,192,192]{3,2,1,0:T(8,128)S(1)}, u32[]{:S(2)}, u32[]{:S(2)}) %collective-permute-start.1) | collective-permute-done | bytes 294944 | tf_op jit(solution)/shard_map/ppermute | solution.py:11
  16.9 0.7 constant_dynamic-update-slice_fusion.62
  19.4 0.7 constant_dynamic-update-slice_fusion.58
  20.7 0.7 constant_dynamic-update-slice_fusion.56
  21.9 0.7 constant_dynamic-update-slice_fusion.54
  23.2 0.7 constant_dynamic-update-slice_fusion.52
  25.7 0.7 constant_dynamic-update-slice_fusion.48
  27.0 0.7 constant_dynamic-update-slice_fusion.46
  28.2 0.7 constant_dynamic-update-slice_fusion.44
  32.0 0.7 constant_dynamic-update-slice_fusion.38
  33.3 0.7 constant_dynamic-update-slice_fusion.36
  34.5 0.7 constant_dynamic-update-slice_fusion.34
  37.0 0.7 constant_dynamic-update-slice_fusion.30
  38.3 0.7 constant_dynamic-update-slice_fusion.28
  40.8 0.7 constant_dynamic-update-slice_fusion.24
  42.1 0.7 constant_dynamic-update-slice_fusion.22
  43.3 0.7 constant_dynamic-update-slice_fusion.20
  44.6 0.7 constant_dynamic-update-slice_fusion.18
  45.8 0.7 constant_dynamic-update-slice_fusion.16
  49.6 0.7 constant_dynamic-update-slice_fusion.10
  53.4 0.7 constant_dynamic-update-slice_fusion.4
  55.9 0.7 constant_dynamic-update-slice_fusion
  56.6 18.8 %all-to-all-start = ((f32[64,1,2,576]{3,2,1,0:T(2,128)}), f32[64,1,2,576]{3,2,1,0:T(2,128)S(1)}, u32[]{:S(2)}, u32[]{:S(2)}) async-start(f32[64,1,2,576]{3,2,1,0:T(2,128)} %constant_dynamic-update-slice_fusion), calls=%async_computation | async-start | bytes 655360 | tf_op jit(solution)/shard_map/all_to_all | solution.py:66
  76.4 23.1 %all-to-all-done = f32[64,1,2,576]{3,2,1,0:T(2,128)S(1)} async-done(((f32[64,1,2,576]{3,2,1,0:T(2,128)}), f32[64,1,2,576]{3,2,1,0:T(2,128)S(1)}, u32[]{:S(2)}, u32[]{:S(2)}) %all-to-all-start) | async-done | bytes 294944 | tf_op jit(solution)/shard_map/all_to_all | solution.py:66
  99.7 0.7 fusion.43
  100.7 0.7 fusion
  101.6 24.2 %all_to_all.20 = bf16[64,2,576]{2,1,0:T(2,128)(2,1)S(1)} all-to-all(bf16[64,2,576]{2,1,0:T(2,128)(2,1)S(1)} %copy.72), channel_id=1, replica_groups=mesh['energy'=64,'slab'=8] {'energy'}, dimensions={0} | all-to-all | bytes 294912 | tf_op jit(solution)/shard_map/all_to_all | solution.py:86
  125.8 0.9 reshape.134
  (81 shorter events, 31.0 us)
Async XLA Ops:
  0.0 7.2 %collective-permute-start = (bf16[1,2,192,192]{3,2,1,0:T(8,128)(2,1)}, bf16[1,2,192,192]{3,2,1,0:T(8,128)(2,1)S(1)}, u32[]{:S(2)}, u32[]{:S(2)}) collective-permute-start(bf16[1,2,192,192]{3,2,1,0:T(8,128)(2,1)} %bitcast.358), channel_id=1, source_target_pairs={{0,1},{1,2},{2,3},{3,4},{4,5},{5,6},{6,7},{8,9},{9,10},{10,11},{11... | collective-permute-start | bytes 442376 | tf_op jit(solution)/shard_map/ppermute | solution.py:11
  1.9 1.2 copy-start
  1.9 1.2 copy-start.1
  8.7 7.2 %collective-permute-start.1 = (f32[1,2,192,192]{3,2,1,0:T(8,128)S(1)}, f32[1,2,192,192]{3,2,1,0:T(8,128)S(1)}, u32[]{:S(2)}, u32[]{:S(2)}) collective-permute-start(f32[1,2,192,192]{3,2,1,0:T(8,128)S(1)} %pad_maximum_fusion), channel_id=1, source_target_pairs={{1,0},{2,1},{3,2},{4,3},{5,4},{6,5},{7,6},{9,8},{10,9},{11,10},{12... | collective-permute-start | bytes 884744 | tf_op jit(solution)/shard_map/ppermute | solution.py:11
  56.6 42.9 %all-to-all-start = ((f32[64,1,2,576]{3,2,1,0:T(2,128)}), f32[64,1,2,576]{3,2,1,0:T(2,128)S(1)}, u32[]{:S(2)}, u32[]{:S(2)}) async-start(f32[64,1,2,576]{3,2,1,0:T(2,128)} %constant_dynamic-update-slice_fusion), calls=%async_computation | async-start | bytes 655360 | tf_op jit(solution)/shard_map/all_to_all | solution.py:66
  99.6 1.0 copy-start.2
